TPU v7x, 512 devices: a whole 4x8x8 slice. The times are simulated.
512 devices in a mesh: dp: 32 (over y, x), tensor: 16 (over z, core).
Axes of the slice: x: 4, y: 8, z: 8, core: 2. Of those that a mesh axis runs over, the one named last changes fastest.
Arguments:
- activations: bfloat16 [90112, 4096], P('dp', 'tensor'), may hold values from -6 to 6
- cotangent: bfloat16 [90112, 4096], P('dp', 'tensor'), may hold values from -6 to 6
- down_adapters: bfloat16 [192, 4096, 64], P('dp', 'tensor'), may hold values from -0.09375 to 0.09375
- up_adapters: bfloat16 [192, 64, 4096], P('dp', None, 'tensor'), may hold values from -0.75 to 0.75
- block_persona: int32 [704], P('dp'), may hold values from 0 to 191, as said below
- persona_slot: int32 [192], replicated, may hold values from 0 to 191, as said below
Outputs:
- grad_input: bfloat16 [90112, 4096], P('dp', 'tensor')
- grad_down: bfloat16 [192, 4096, 64], P('dp', 'tensor')
- grad_up: bfloat16 [192, 64, 4096], P('dp', None, 'tensor')
Inputs may be any that keep to these rules, and one draw needn't show every extreme that they name: `block_persona`: among the 22 blocks of one index of dp, at most 2 name personas of one owner; in every draw one owner gets exactly 2 blocks from every index of dp. `persona_slot`: A permutation of the slots.
All inputs are finite; a program needn't handle non-finite values.
Results may differ from a plain program's by a relative error of at most 0.005.
Values may be sent and summed in bfloat16 or wider, within the bound.
A program may use at most 64 MiB of HBM per device.

v0:
```python
import jax
import jax.numpy as jnp
from jax import lax
from jax.sharding import PartitionSpec as P

adapter_scale = 2.0


def shards(activations, cotangent, down_adapters, up_adapters, block_persona, persona_slot):
    holder_count = lax.axis_size("dp")
    block_count = block_persona.shape[0]
    rows_per_block = activations.shape[0] // block_count
    feature_columns = activations.shape[1]
    adapter_rank = down_adapters.shape[2]
    persona_count = down_adapters.shape[0]
    slot_capacity = max(2, block_count // holder_count + 1)
    number_of_slots = holder_count * slot_capacity
    persona_ids = jnp.arange(persona_slot.shape[0], dtype=jnp.int32)
    slot_of_block = jnp.sum(
        jnp.where(block_persona[:, None] == persona_ids[None, :], persona_slot[None, :], 0), axis=1
    )
    owners = slot_of_block // persona_count
    local_index = slot_of_block % persona_count
    same_owner = owners[:, None] == owners[None, :]
    block_ids = jnp.arange(block_count, dtype=jnp.int32)
    earlier = block_ids[:, None] > block_ids[None, :]
    position = jnp.sum(jnp.logical_and(same_owner, earlier).astype(jnp.int32), axis=1)
    target = owners * slot_capacity + position
    placing = target[None, :] == jnp.arange(number_of_slots, dtype=jnp.int32)[:, None]
    requests = jnp.sum(jnp.where(placing, local_index[None, :] + 1, 0), axis=1) - 1
    placing_half = placing.astype(jnp.bfloat16)
    act_blocks = activations.reshape(block_count, rows_per_block, feature_columns)
    cot_blocks = cotangent.reshape(block_count, rows_per_block, feature_columns)
    received_ids = lax.all_to_all(
        requests.reshape(holder_count, slot_capacity), "dp", split_axis=0, concat_axis=0, tiled=True
    ).reshape(number_of_slots)
    clamped_index = jnp.maximum(received_ids, 0)
    selected_down = down_adapters[clamped_index].reshape(
        holder_count, slot_capacity, feature_columns, adapter_rank
    )
    selected_up = up_adapters[clamped_index].reshape(
        holder_count, slot_capacity, adapter_rank, feature_columns
    )
    down_gradient, up_gradient = (
        lax.all_to_all(selected_down, "dp", split_axis=0, concat_axis=0, tiled=True),
        lax.all_to_all(selected_up, "dp", split_axis=0, concat_axis=0, tiled=True),
    )
    slotted_down = down_gradient.reshape(number_of_slots, feature_columns, adapter_rank)
    slotted_up = up_gradient.reshape(number_of_slots, adapter_rank, feature_columns)
    down_blocks = jnp.einsum(
        "sb,sdr->bdr", placing_half, slotted_down, preferred_element_type=jnp.float32
    ).astype(jnp.bfloat16)
    up_blocks = jnp.einsum(
        "sb,srd->brd", placing_half, slotted_up, preferred_element_type=jnp.float32
    ).astype(jnp.bfloat16)
    part_up = jnp.einsum(
        "btd,bdr->btr", act_blocks, down_blocks, preferred_element_type=jnp.float32
    )
    part_back = jnp.einsum(
        "btd,brd->btr", cot_blocks, up_blocks, preferred_element_type=jnp.float32
    )
    summed_up, summed_back = lax.psum((part_up, part_back), "tensor")
    rank_up = summed_up.astype(jnp.bfloat16)
    rank_gradient = summed_back.astype(jnp.bfloat16)
    grad_input = (
        adapter_scale
        * jnp.einsum("btr,bdr->btd", rank_gradient, down_blocks, preferred_element_type=jnp.float32)
    ).astype(jnp.bfloat16)
    grad_input = grad_input.reshape(activations.shape)
    block_down = jnp.einsum(
        "btd,btr->bdr", act_blocks, rank_gradient, preferred_element_type=jnp.float32
    )
    block_up = jnp.einsum("btr,btd->brd", rank_up, cot_blocks, preferred_element_type=jnp.float32)
    placing_full = placing.astype(jnp.float32)
    per_slot_down = jnp.einsum(
        "sb,bdr->sdr", placing_full, block_down, precision=lax.Precision.HIGHEST
    )
    per_slot_up = jnp.einsum("sb,brd->srd", placing_full, block_up, precision=lax.Precision.HIGHEST)
    returned_down, returned_up = (
        lax.all_to_all(
            per_slot_down.reshape(holder_count, slot_capacity, feature_columns, adapter_rank),
            "dp",
            split_axis=0,
            concat_axis=0,
            tiled=True,
        ),
        lax.all_to_all(
            per_slot_up.reshape(holder_count, slot_capacity, adapter_rank, feature_columns),
            "dp",
            split_axis=0,
            concat_axis=0,
            tiled=True,
        ),
    )
    holder_down = returned_down.reshape(number_of_slots, feature_columns, adapter_rank)
    holder_up = returned_up.reshape(number_of_slots, adapter_rank, feature_columns)
    member_ids = jnp.arange(persona_count, dtype=jnp.int32)
    chosen_map = (received_ids[:, None] == member_ids[None, :]).astype(jnp.float32)
    member_counts = jnp.sum(chosen_map, axis=0)
    scaling_multiplier = adapter_scale / (rows_per_block * jnp.maximum(member_counts, 1.0))
    grad_down = (
        jnp.einsum("sp,sdr->pdr", chosen_map, holder_down, precision=lax.Precision.HIGHEST)
        * scaling_multiplier[:, None, None]
    ).astype(jnp.bfloat16)
    grad_up = (
        jnp.einsum("sp,srd->prd", chosen_map, holder_up, precision=lax.Precision.HIGHEST)
        * scaling_multiplier[:, None, None]
    ).astype(jnp.bfloat16)
    return (grad_input, grad_down, grad_up)


def solution(mesh):
    return jax.shard_map(
        shards,
        mesh=mesh,
        in_specs=(
            P("dp", "tensor"),
            P("dp", "tensor"),
            P("dp", "tensor", None),
            P("dp", None, "tensor"),
            P("dp"),
            P(),
        ),
        out_specs=(P("dp", "tensor"), P("dp", "tensor", None), P("dp", None, "tensor")),
        check_vma=False,
    )
```

profile of v0, /device:TPU:195, one launch (start us, length us, event | category | flops | bytes accessed | tf_op | source)
XLA Modules:
  0.0 449.8 jit_solution(5014778337699437248)
XLA Ops:
  0.6 1.0 select_reduce_fusion
  1.6 0.2 convert_reduce_fusion
  1.9 0.4 copy-done.6
  2.5 17.1 %all_to_all.26 = s32[32,1,2]{2,1,0:T(1,128)S(1)} all-to-all(s32[32,1,2]{2,1,0:T(1,128)S(1)} %bitcast.52), channel_id=1, replica_groups=mesh['dp'=32,'tensor'=16] {'dp'}, dimensions={0} | all-to-all | bytes 512 | tf_op jit(solution)/shard_map/all_to_all | solution.py:34
  19.6 0.5 broadcast.167
  20.1 0.7 fusion.28
  21.0 0.6 pad_clamp_fusion
  21.6 1.7 gather_fusion.1
  23.3 3.5 copy.97
  26.8 5.6 %all-to-all-start.2 = ((bf16[32,2,256,64]{2,1,3,0:T(2,128)(2,1)}), bf16[32,2,256,64]{2,1,3,0:T(2,128)(2,1)}, u32[]{:S(2)}, u32[]{:S(2)}) async-start(bf16[32,2,256,64]{2,1,3,0:T(2,128)(2,1)} %copy.97), calls=%async_computation.2 | async-start | bytes 4194304 | tf_op jit(solution)/shard_map/all_to_all | solution.py:45
  32.5 2.1 gather_fusion
  34.6 5.1 %copy.94 = bf16[32,2,64,256]{3,1,2,0:T(2,128)(2,1)} copy(bf16[32,2,64,256]{3,2,1,0:T(8,128)(2,1)} %bitcast.48) | data formatting | bytes 4194304 | tf_op jit(solution)/shard_map/reshape | solution.py:41
  39.8 40.3 %all-to-all-done.2 = bf16[32,2,256,64]{2,1,3,0:T(2,128)(2,1)} async-done(((bf16[32,2,256,64]{2,1,3,0:T(2,128)(2,1)}), bf16[32,2,256,64]{2,1,3,0:T(2,128)(2,1)}, u32[]{:S(2)}, u32[]{:S(2)}) %all-to-all-start.2) | async-done | bytes 2097184 | tf_op jit(solution)/shard_map/all_to_all | solution.py:45
  80.1 6.7 %all-to-all-start.1 = ((bf16[32,2,64,256]{3,1,2,0:T(2,128)(2,1)}), bf16[32,2,64,256]{3,1,2,0:T(2,128)(2,1)S(1)}, u32[]{:S(2)}, u32[]{:S(2)}) async-start(bf16[32,2,64,256]{3,1,2,0:T(2,128)(2,1)} %copy.94), calls=%async_computation.1 | async-start | bytes 4194304 | tf_op jit(solution)/shard_map/all_to_all | solution.py:46
  86.8 5.2 %copy.98 = bf16[32,2,256,64]{2,1,0,3:T(2,128)(2,1)} copy(bf16[32,2,256,64]{2,1,3,0:T(2,128)(2,1)} %all-to-all-done.2) | data formatting | bytes 4194304 | tf_op jit(solution)/shard_map/all_to_all | solution.py:45
  92.1 4.1 reshape.116
  96.2 3.0 fusion.14
  99.1 35.9 %all-to-all-done.1 = bf16[32,2,64,256]{3,1,2,0:T(2,128)(2,1)S(1)} async-done(((bf16[32,2,64,256]{3,1,2,0:T(2,128)(2,1)}), bf16[32,2,64,256]{3,1,2,0:T(2,128)(2,1)S(1)}, u32[]{:S(2)}, u32[]{:S(2)}) %all-to-all-start.1) | async-done | bytes 2097184 | tf_op jit(solution)/shard_map/all_to_all | solution.py:46
  135.1 3.7 copy.95
  138.7 2.7 reshape.113
  141.5 1.2 convolution_convert_fusion
  142.8 0.1 copy-done.4
  142.9 0.6 convolution_bitcast_fusion.2
  143.5 0.4 copy-done.3
  143.9 1.5 convolution_bitcast_fusion.1
  145.4 61.6 %all-reduce.2 = (bf16[22,128,64]{1,2,0:T(8,128)(2,1)S(1)}, bf16[22,128,64]{1,2,0:T(8,128)(2,1)}) all-reduce(f32[22,128,64]{1,2,0:T(8,128)S(1)} %convolution_bitcast_fusion.2, f32[22,128,64]{1,2,0:T(8,128)} %convolution_bitcast_fusion.1), channel_id=1, replica_groups=mesh['dp'=32,'tensor'=16] {'tensor'}, use_global_device_ids=true, to_apply=%region_3.4 | all-reduce | flops 360448 | bytes 2162688 | tf_op jit(solution)/shard_map/psum | solution.py:62
  207.0 0.4 convolution_bitcast_fusion
  207.4 4.7 %fusion.2 = f32[64,256,64]{1,0,2:T(8,128)} fusion(f32[22,256,64]{1,2,0:T(8,128)S(1)} %convolution_bitcast_fusion, s32[22]{0:T(128)S(1)} %copy-done.7), kind=kOutput, calls=%fused_computation.5 | convolution fusion | flops 276825472 | bytes 5636184 | tf_op jit(solution)/shard_map/sb,bdr->sdr/dot_general | solution.py:75
  212.0 5.8 %reshape.119 = f32[32,2,256,64]{2,1,0,3:T(2,128)} reshape(f32[64,256,64]{1,0,2:T(8,128)} %fusion.2) | data formatting | bytes 8388608 | tf_op jit(solution)/shard_map/reshape | solution.py:81
  217.9 6.5 %copy.101 = f32[32,2,256,64]{2,1,3,0:T(2,128)} copy(f32[32,2,256,64]{2,1,0,3:T(2,128)} %reshape.119) | data formatting | bytes 8388608 | tf_op jit(solution)/shard_map/reshape | solution.py:81
  224.4 5.9 %all-to-all-start.3 = ((f32[32,2,256,64]{2,1,3,0:T(2,128)}), f32[32,2,256,64]{2,1,3,0:T(2,128)}, u32[]{:S(2)}, u32[]{:S(2)}) async-start(f32[32,2,256,64]{2,1,3,0:T(2,128)} %copy.101), calls=%async_computation.3 | async-start | bytes 8388608 | tf_op jit(solution)/shard_map/all_to_all | solution.py:80
  230.3 1.7 fusion.29
  232.0 4.7 %fusion = f32[64,64,256]{2,0,1:T(8,128)} fusion(f32[22,64,256]{2,1,0:T(8,128)S(1)} %fusion.29, s32[22]{0:T(128)S(1)} %copy-done.7), kind=kOutput, calls=%fused_computation.3 | convolution fusion | flops 276825472 | bytes 5636184 | tf_op jit(solution)/shard_map/sb,brd->srd/dot_general | solution.py:78
  236.6 5.8 %reshape.121 = f32[32,2,64,256]{3,1,0,2:T(2,128)} reshape(f32[64,64,256]{2,0,1:T(8,128)} %fusion) | data formatting | bytes 8388608 | tf_op jit(solution)/shard_map/reshape | solution.py:88
  242.5 6.5 %copy.104 = f32[32,2,64,256]{3,1,2,0:T(2,128)} copy(f32[32,2,64,256]{3,1,0,2:T(2,128)} %reshape.121) | data formatting | bytes 8388608 | tf_op jit(solution)/shard_map/reshape | solution.py:88
  249.0 80.8 %all-to-all-done.3 = f32[32,2,256,64]{2,1,3,0:T(2,128)} async-done(((f32[32,2,256,64]{2,1,3,0:T(2,128)}), f32[32,2,256,64]{2,1,3,0:T(2,128)}, u32[]{:S(2)}, u32[]{:S(2)}) %all-to-all-start.3) | async-done | bytes 4194336 | tf_op jit(solution)/shard_map/all_to_all | solution.py:80
  329.8 5.5 %all-to-all-start.4 = ((f32[32,2,64,256]{3,1,2,0:T(2,128)}), f32[32,2,64,256]{3,1,2,0:T(2,128)}, u32[]{:S(2)}, u32[]{:S(2)}) async-start(f32[32,2,64,256]{3,1,2,0:T(2,128)} %copy.104), calls=%async_computation.4 | async-start | bytes 8388608 | tf_op jit(solution)/shard_map/all_to_all | solution.py:87
  335.4 0.1 convert_reduce_fusion.1
  335.5 1.7 multiply_convert_fusion
  337.2 6.5 %copy.102 = f32[32,2,256,64]{2,1,0,3:T(2,128)} copy(f32[32,2,256,64]{2,1,3,0:T(2,128)} %all-to-all-done.3) | data formatting | bytes 8388608 | tf_op jit(solution)/shard_map/all_to_all | solution.py:80
  343.7 6.1 %reshape.120 = f32[64,256,64]{1,0,2:T(8,128)} reshape(f32[32,2,256,64]{2,1,0,3:T(2,128)} %copy.102) | data formatting | bytes 8388608 | tf_op jit(solution)/shard_map/reshape | solution.py:95
  349.8 3.6 fusion.4
  353.4 0.7 copy.106
  354.2 78.6 %all-to-all-done.4 = f32[32,2,64,256]{3,1,2,0:T(2,128)} async-done(((f32[32,2,64,256]{3,1,2,0:T(2,128)}), f32[32,2,64,256]{3,1,2,0:T(2,128)}, u32[]{:S(2)}, u32[]{:S(2)}) %all-to-all-start.4) | async-done | bytes 4194336 | tf_op jit(solution)/shard_map/all_to_all | solution.py:87
  432.8 6.5 %copy.105 = f32[32,2,64,256]{3,1,0,2:T(2,128)} copy(f32[32,2,64,256]{3,1,2,0:T(2,128)} %all-to-all-done.4) | data formatting | bytes 8388608 | tf_op jit(solution)/shard_map/all_to_all | solution.py:87
  439.3 6.2 %reshape.122 = f32[64,64,256]{2,0,1:T(8,128)} reshape(f32[32,2,64,256]{3,1,0,2:T(2,128)} %copy.105) | data formatting | bytes 8388608 | tf_op jit(solution)/shard_map/reshape | solution.py:96
  445.4 3.6 fusion.5
  449.1 0.7 copy.107
  (21 shorter events, 0.5 us)
Async XLA Ops:
  0.6 142.9 %copy-start = (bf16[2816,256]{1,0:T(8,128)(2,1)S(1)}, bf16[2816,256]{1,0:T(8,128)(2,1)}, u32[]{:S(2)}) copy-start(bf16[2816,256]{1,0:T(8,128)(2,1)} %param.6) | copy-start | bytes 4325380
  1.8 0.5 copy-start.6
  26.8 5.6 %copy-start.2 = (bf16[6,64,256]{2,1,0:T(8,128)(2,1)S(1)}, bf16[6,64,256]{2,1,0:T(8,128)(2,1)}, u32[]{:S(2)}) copy-start(bf16[6,64,256]{2,1,0:T(8,128)(2,1)} %param.9) | copy-start | bytes 589828
  26.8 53.3 %all-to-all-start.2 = ((bf16[32,2,256,64]{2,1,3,0:T(2,128)(2,1)}), bf16[32,2,256,64]{2,1,3,0:T(2,128)(2,1)}, u32[]{:S(2)}, u32[]{:S(2)}) async-start(bf16[32,2,256,64]{2,1,3,0:T(2,128)(2,1)} %copy.97), calls=%async_computation.2 | async-start | bytes 4194304 | tf_op jit(solution)/shard_map/all_to_all | solution.py:45
  80.1 55.0 %all-to-all-start.1 = ((bf16[32,2,64,256]{3,1,2,0:T(2,128)(2,1)}), bf16[32,2,64,256]{3,1,2,0:T(2,128)(2,1)S(1)}, u32[]{:S(2)}, u32[]{:S(2)}) async-start(bf16[32,2,64,256]{3,1,2,0:T(2,128)(2,1)} %copy.94), calls=%async_computation.1 | async-start | bytes 4194304 | tf_op jit(solution)/shard_map/all_to_all | solution.py:46
  141.5 1.4 copy-start.4
  142.7 1.1 copy-start.3
  145.4 62.0 %copy-start.7 = (s32[22]{0:T(128)S(1)}, s32[22]{0:T(128)}, u32[]{:S(2)}) copy-start(s32[22]{0:T(128)} %copy-done.6) | copy-start | bytes 268
  224.4 5.9 %copy-start.5 = (bf16[22,128,64]{1,2,0:T(8,128)(2,1)S(1)}, bf16[22,128,64]{1,2,0:T(8,128)(2,1)}, u32[]{:S(2)}) copy-start(bf16[22,128,64]{1,2,0:T(8,128)(2,1)} %get-tuple-element.30) | copy-start | bytes 1081348
  224.4 105.4 %all-to-all-start.3 = ((f32[32,2,256,64]{2,1,3,0:T(2,128)}), f32[32,2,256,64]{2,1,3,0:T(2,128)}, u32[]{:S(2)}, u32[]{:S(2)}) async-start(f32[32,2,256,64]{2,1,3,0:T(2,128)} %copy.101), calls=%async_computation.3 | async-start | bytes 8388608 | tf_op jit(solution)/shard_map/all_to_all | solution.py:80
  329.8 103.0 %all-to-all-start.4 = ((f32[32,2,64,256]{3,1,2,0:T(2,128)}), f32[32,2,64,256]{3,1,2,0:T(2,128)}, u32[]{:S(2)}, u32[]{:S(2)}) async-start(f32[32,2,64,256]{3,1,2,0:T(2,128)} %copy.104), calls=%async_computation.4 | async-start | bytes 8388608 | tf_op jit(solution)/shard_map/all_to_all | solution.py:87
  439.3 10.5 %copy-start.1 = (bf16[2816,256]{1,0:T(8,128)(2,1)S(1)}, bf16[2816,256]{1,0:T(8,128)(2,1)}, u32[]{:S(2)}) copy-start(bf16[2816,256]{1,0:T(8,128)(2,1)} %param.6) | copy-start | bytes 4325380
where the time goes:
time: 451 us; the launch traced here: 450 us
  waiting for transfers between devices  236 us (52%)
  local copies, waits for them, and re-layouts  81.4 us (18%)
  blocking collectives  78.8 us (17%)
  matrix products  26.7 us (6%)
  starting transfers between devices  23.7 us (5%)
    all_to_all x1, waiting for transfers between devices, shards(): lax.all_to_all(per_slot_down.reshape(holder_count, slot_capacity, feature...  80.8 us
    all_to_all x1, waiting for transfers between devices, shards(): lax.all_to_all(per_slot_up.reshape(holder_count, slot_capacity, adapter_r...  78.6 us
    psum x1, blocking collectives, shards(): summed_up, summed_back = lax.psum((part_up, part_back), 'tensor')  61.6 us
    all_to_all x1, waiting for transfers between devices, shards(): lax.all_to_all(selected_down, 'dp', split_axis=0, concat_axis=0, tiled=True)  40.3 us
    all_to_all x1, waiting for transfers between devices, shards(): lax.all_to_all(selected_up, 'dp', split_axis=0, concat_axis=0, tiled=True)  35.9 us
    all_to_all x1, blocking collectives, shards(): lax.all_to_all(requests.reshape(holder_count, slot_capacity), 'dp', split...  17.1 us
    reshape x2, local copies, waits for them, and re-layouts, shards(): per_slot_up.reshape(holder_count, slot_capacity, adapter_rank, feature_co...  12.3 us
    reshape x2, local copies, waits for them, and re-layouts, shards(): per_slot_down.reshape(holder_count, slot_capacity, feature_columns, adapt...  12.3 us
  transfers between devices with their start and end apart: 4, of which 4 were waited for; matrix products, arithmetic and copies ran while one was open for 13% of the time, Pallas kernels for 0%

commit v1 on v0

v1 whole, which is shorter than its diff:
```python
import functools

import jax
import jax.numpy as jnp
from jax import lax
from jax.experimental import pallas as pl
from jax.experimental.pallas import tpu as pltpu
from jax.sharding import PartitionSpec as P

MESH = pl.DeviceIdType.MESH
NX = 4
CORES = 2
CAP = 2
ADAPTER_SCALE = 2.0
F32 = jnp.float32
BF16 = jnp.bfloat16


def prep_kernel(ny, pers, blocks, bp, ps, req, blk_slot, slot_blk, used):
    me = lax.axis_index("dp")
    my_y, my_x = me // NX, me % NX
    owners = ny * NX

    def clear(i, _):
        req[0, i] = -1
        slot_blk[0, i] = blocks
        used[i] = 0
        return 0

    lax.fori_loop(0, 128, clear, 0)

    def place(b, _):
        slot = ps[bp[b]]
        owner = slot // pers
        pos = used[owner]
        used[owner] = pos + 1
        s = owner * CAP + pos
        req[0, s] = slot - owner * pers
        slot_blk[0, s] = b
        row = lax.rem(owner // NX - my_y + ny, ny)
        rel = lax.rem(lax.rem(owner, NX) - my_x + NX, NX)
        own = 8 * ny + row * 2 + pos
        right = 3 * ny + row * 3 + pos
        left = row * 3 + pos
        across = 6 * ny + pos * ny + row
        blk_slot[0, b] = jnp.where(
            rel == 0, own, jnp.where(rel == 1, right, jnp.where(rel == 2, across, left))
        )
        return 0

    lax.fori_loop(0, blocks, place, 0)


class Copies:
    def __init__(self, send, recv):
        self.send, self.recv, self.used, self.all = send, recv, 0, []

    def make(self, src, dst, device):
        i = self.used
        self.used += 1
        copy = pltpu.make_async_remote_copy(
            src_ref=src, dst_ref=dst, send_sem=self.send.at[i], recv_sem=self.recv.at[i],
            device_id=device, device_id_type=MESH,
        )
        self.all.append(copy)
        return copy


def copy_count(ny, nz):
    return 2 * ny * 4 * 2 + 2 * (ny - 1) * 2 + 2 * (2 + 2 * (nz - 1)) + (NX - 1) + (ny - 1)


def main_kernel(cfg, *refs):
    ny, nz, pers, blocks, pad_blocks, rank = cfg
    (req_s, blk_slot, slot_blk, req_v, up, down, act, cot, gi, gdn, gup) = refs[:11]
    refs = list(refs[11:])

    def take(n):
        out = refs[:n]
        del refs[:n]
        return out

    act_v, cot_v, gi_v = take(3)
    tab = [[up] + take(ny - 1), take(ny)]
    rx = take(2)
    sx = [take(2), take(2)]
    grads = take(2)
    gr = take(2)
    bs = [take(2), take(2)]
    ys = [take(ny - 1), take(ny - 1)]
    yr = [take(ny - 1), take(ny - 1)]
    part, pair, zs, zr, full = take(2), take(2), take(2), take(2), take(2)
    rtab_v, rtab_s, ctab = take(3)
    send_sem, recv_sem, local_sem = take(3)
    copies = Copies(send_sem, recv_sem)

    dp, tensor = lax.axis_index("dp"), lax.axis_index("tensor")
    y, x = dp // NX, lax.rem(dp, NX)
    z, core = tensor // CORES, lax.rem(tensor, CORES)

    def at_x(d):
        return (y * NX + lax.rem(x + d + NX, NX), tensor)

    def at_y(d):
        return (lax.rem(y + d + ny, ny) * NX + x, tensor)

    def at_z(d):
        return (dp, lax.rem(z + d + nz, nz) * CORES + core)

    sibling = (dp, z * CORES + (1 - core))

    load_act = pltpu.make_async_copy(act, act_v, local_sem.at[0])
    load_cot = pltpu.make_async_copy(cot, cot_v, local_sem.at[1])
    load_act.start()
    load_cot.start()

    barrier = pltpu.get_barrier_semaphore()
    peers = [at_x(d) for d in range(1, NX)] + [at_y(d) for d in range(1, ny)]
    peers += [at_z(d) for d in range(1, nz)] + [sibling]
    for peer in peers:
        pl.semaphore_signal(barrier, inc=1, device_id=peer, device_id_type=MESH)
    pl.semaphore_wait(barrier, len(peers))

    steps_p = [ny // 2, ny - 1 - ny // 2]
    steps_m = [ny - 1 - ny // 2, ny // 2]
    ring = {}

    def ring_send(h, toward_low, step):
        if toward_low:
            src, row, device = tab[h][step - 1], step, at_y(-1)
        else:
            src, row, device = tab[h][(ny - step + 1) % ny], ny - step, at_y(1)
        copy = copies.make(src, tab[h][row], device)
        copy.start()
        ring[h, row] = (copy, toward_low, step)

    def ring_first(h, toward_low):
        if (steps_p if toward_low else steps_m)[h] >= 1:
            ring_send(h, toward_low, 1)

    def ring_take(h, row):
        if row == 0:
            return
        copy, toward_low, step = ring[h, row]
        copy.wait_recv()
        if step < (steps_p if toward_low else steps_m)[h]:
            ring_send(h, toward_low, step + 1)
        elif h == 0:
            ring_first(1, toward_low)

    def ring_order(h):
        order = [0]
        for s in range(1, ny // 2 + 1):
            first = [(s, steps_p[h]), (ny - s, steps_m[h])]
            order += [row for row, steps in first if s <= steps]
        return order

    ask = []
    for d in range(1, NX):
        copy = copies.make(req_v, rtab_v.at[NX - d], at_x(d))
        copy.start()
        ask.append(copy)
    ring_first(0, True)
    ring_first(0, False)
    if steps_m[0] == 0:
        ring_first(1, False)
    rtab_v[0] = req_v[...]

    for k in range(pers):
        tab[1][0][k] = jnp.transpose(down[k])

    for copy in ask:
        copy.wait_recv()
    to_smem = pltpu.make_async_copy(rtab_v, rtab_s, local_sem.at[2])
    to_smem.start()
    ctab[0] = rtab_v[...]
    to_smem.wait()
    table_copies = []
    for d in range(1, ny):
        copy = copies.make(rtab_v, ctab.at[ny - d], at_y(d))
        copy.start()
        table_copies.append(copy)

    def owner_slot(row, rel_x):
        return (lax.rem(y + row, ny) * NX + lax.rem(x + rel_x, NX)) * CAP

    hops = {}

    def x_send(key, land, stage, row):
        for side, d in ((0, 1), (1, -1)):
            copy = copies.make(
                stage[side].at[row], land.at[pl.ds(side * 3 * ny + row * 3, 3)], at_x(d)
            )
            copy.start()
            hops[key, side] = copy

    def x_hand_on(key, land, row):
        for side, d in ((0, 1), (1, -1)):
            hops[key, side].wait_recv()
            copy = copies.make(
                land.at[pl.ds(side * 3 * ny + row * 3 + 2, 1)],
                land.at[pl.ds((6 + side) * ny + row, 1)],
                at_x(d),
            )
            copy.start()
            hops[key, side + 2] = copy

    def x_landed(key):
        hops[key, 2].wait_recv()
        hops[key, 3].wait_recv()

    def issue_adapters(h, row):
        table = tab[h][row]

        def pick(rel_x, pos):
            return table[jnp.maximum(rtab_s[rel_x, 0, owner_slot(row, 0) + pos], 0)]

        for side, rel_x in ((0, 1), (1, NX - 1)):
            stage = sx[h][side]
            stage[row, 0] = pick(rel_x, 0)
            stage[row, 1] = pick(rel_x, 1)
            stage[row, 2] = pick(2, side)
        x_send(("a", h, row), rx[h], sx[h], row)
        for pos in range(CAP):
            rx[h][8 * ny + row * 2 + pos] = pick(0, pos)

    def issue_gradients(h, row):
        def pick(rel_x, pos):
            return grads[h][slot_blk[0, owner_slot(row, rel_x) + pos]]

        for side, rel_x in ((0, 1), (1, NX - 1)):
            stage = bs[h][side]
            stage[row, 0] = pick(rel_x, 0)
            stage[row, 1] = pick(rel_x, 1)
            stage[row, 2] = pick(2, side)
        x_send(("g", h, row), gr[h], bs[h], row)

    sums = {}

    def row_sum(h, row, k):
        base = owner_slot(row, 0)
        total = jnp.zeros((rank, up.shape[2]), F32)
        places = [(3, row * 3), (1, 3 * ny + row * 3)]
        terms = []
        for rel_x, first in places:
            for pos in range(CAP):
                terms.append((rtab_s[rel_x, 0, base + pos], gr[h][first + pos]))
        terms.append((rtab_s[2, 0, base], gr[h][6 * ny + row]))
        terms.append((rtab_s[2, 0, base + 1], gr[h][7 * ny + row]))
        for pos in range(CAP):
            terms.append((rtab_s[0, 0, base + pos], grads[h][slot_blk[0, base + pos]]))
        for asked, term in terms:
            total += jnp.where(asked == k, term.astype(F32), 0.0)
        return total

    back_p = [steps_p[1], steps_p[0]]
    back_m = [steps_m[1], steps_m[0]]

    def back_place(h, row):
        j = ny - row
        return (True, j) if j <= back_p[h] else (False, row)

    def back_slot(toward_low, j):
        return j - 1 if toward_low else ny - 1 - j

    def back_order(h):
        order = []
        for j in range(ny // 2, 0, -1):
            order += [ny - j] if j <= back_p[h] else []
            order += [j] if j <= back_m[h] else []
        return order + [0]

    def finish_gradients(h, row):
        x_landed(("g", h, row))
        if row == 0:
            return
        toward_low, j = back_place(h, row)
        farther = None
        if j < (back_p if toward_low else back_m)[h]:
            sums[h, toward_low, j + 1].wait_recv()
            farther = yr[h][back_slot(toward_low, j + 1)]
        out = ys[h][back_slot(toward_low, j)]

        def one(k, _):
            total = row_sum(h, row, k)
            if farther is not None:
                total += farther[k].astype(F32)
            out[k] = total.astype(BF16)
            return 0

        lax.fori_loop(0, pers, one, 0)
        copy = copies.make(out, yr[h][back_slot(toward_low, j)], at_y(-1 if toward_low else 1))
        copy.start()
        sums[h, toward_low, j] = copy

    def write_gradients(h):
        nearest = []
        for toward_low in (True, False):
            if (back_p if toward_low else back_m)[h] >= 1:
                sums[h, toward_low, 1].wait_recv()
                nearest.append(yr[h][back_slot(toward_low, 1)])
        lane = lax.broadcasted_iota(jnp.int32, (1, 128), 1)
        mine = lane // CAP == dp
        for k in range(pers):
            hits = jnp.zeros((1, 128), F32)
            for other in range(ny):
                for rel_x in range(NX):
                    hits += jnp.where(mine & (ctab[other, rel_x] == k), 1.0, 0.0)
            count = jnp.sum(hits, axis=1, keepdims=True)
            scaling = ADAPTER_SCALE / (act.shape[1] * jnp.maximum(count, 1.0))
            total = row_sum(h, 0, k)
            for ref in nearest:
                total += ref[k].astype(F32)
            total = total * scaling
            if h == 0:
                gdn[k] = jnp.transpose(total).astype(BF16)
            else:
                gup[k] = total.astype(BF16)

    half = pad_blocks * rank // 2
    chunk = half // nz
    tensor_copies = {}

    def rows_of(c, zz):
        return pl.ds(pl.multiple_of(c * half + zz * chunk, 16), chunk)

    def project(h):
        if h == 0:
            load_cot.wait()
        for row in range(ny):
            x_landed(("a", h, row))
        tokens = cot_v if h == 0 else act_v

        def one(b, _):
            weights = rx[h][blk_slot[0, b]]
            part[h][pl.ds(pl.multiple_of(b * rank, rank), rank), :] = lax.dot_general(
                weights, tokens[b], (((1,), (1,)), ((), ())), preferred_element_type=F32
            )
            return 0

        lax.fori_loop(0, blocks, one, 0, unroll=2)
        if pad_blocks > blocks:
            part[h][pl.ds(blocks * rank, (pad_blocks - blocks) * rank), :] = jnp.zeros(
                ((pad_blocks - blocks) * rank, part[h].shape[1]), F32
            )
        copy = copies.make(
            part[h].at[pl.ds(pl.multiple_of((1 - core) * half, 16), half)], pair[h], sibling
        )
        copy.start()
        tensor_copies[h, "pair"] = copy

    def scatter(h):
        tensor_copies[h, "pair"].wait_recv()

        def one(zz, _):
            rows = pl.ds(pl.multiple_of(zz * chunk, 16), chunk)
            zs[h][rows, :] = (part[h][rows_of(core, zz), :] + pair[h][rows, :]).astype(BF16)
            return 0

        lax.fori_loop(0, nz, one, 0)
        for d in range(1, nz):
            other = lax.rem(z + d, nz)
            copy = copies.make(
                zs[h].at[pl.ds(pl.multiple_of(other * chunk, 16), chunk)], zr[h].at[d - 1], at_z(d)
            )
            copy.start()
            tensor_copies[h, "scatter", d] = copy

    def gather(h):
        own = pl.ds(pl.multiple_of(z * chunk, 16), chunk)
        total = part[h][rows_of(core, z), :] + pair[h][own, :]
        for d in range(1, nz):
            tensor_copies[h, "scatter", d].wait_recv()
            total += zr[h][d - 1].astype(F32)
        mine = rows_of(core, z)
        full[h][mine, :] = total.astype(BF16)
        for d in range(1, nz):
            copy = copies.make(full[h].at[mine], full[h].at[mine], at_z(d))
            copy.start()
            tensor_copies[h, "gather", d] = copy

    def share(h):
        for d in range(1, nz):
            tensor_copies[h, "gather", d].wait_recv()
        mine = pl.ds(pl.multiple_of(core * half, 16), half)
        copy = copies.make(full[h].at[mine], full[h].at[mine], sibling)
        copy.start()
        tensor_copies[h, "share"] = copy

    def ranks(h, b):
        return full[h][pl.ds(pl.multiple_of(b * rank, rank), rank), :]

    def block_gradients(h):
        tensor_copies[h, "share"].wait_recv()
        if h == 0:
            load_act.wait()
        tokens = act_v if h == 0 else cot_v
        grads[h][blocks] = jnp.zeros(grads[h].shape[1:], BF16)

        def one(b, _):
            grads[h][b] = jnp.dot(ranks(h, b), tokens[b], preferred_element_type=F32).astype(BF16)
            return 0

        lax.fori_loop(0, blocks, one, 0, unroll=2)

    store_gi = pltpu.make_async_copy(gi_v, gi, local_sem.at[3])

    def input_gradient():
        def one(b, _):
            weights = rx[1][blk_slot[0, b]]
            gi_v[b] = (
                ADAPTER_SCALE
                * lax.dot_general(
                    ranks(0, b), weights, (((0,), (0,)), ((), ())), preferred_element_type=F32
                )
            ).astype(BF16)
            return 0

        lax.fori_loop(0, blocks, one, 0, unroll=2)
        store_gi.start()

    jobs = [("a", h, row) for h in (0, 1) for row in ring_order(h)]
    jobs += [("g", h, row) for h in (0, 1) for row in back_order(h)]
    lead, lag, finish_lag = 2, 1, 2
    hooks = {}

    def hook(i, *what):
        hooks.setdefault(i, []).extend(what)

    for h, start in ((0, ny), (1, 2 * ny)):
        stages = [project, scatter, gather, share]
        for j, stage in enumerate(stages):
            hook(start + 2 + (ny - 2) * j // len(stages), functools.partial(stage, h))
            if h == 1 and j == 1:
                hook(start + 2 + (ny - 2) * j // len(stages), input_gradient)
        hook(start + ny, functools.partial(block_gradients, h))
    hook(3 * ny + finish_lag, lambda: write_gradients(0))

    taken = 0
    for i in range(len(jobs) + finish_lag):
        while taken < min(i + lead + 1, 2 * ny):
            ring_take(*jobs[taken][1:])
            taken += 1
        for what in hooks.get(i, []):
            what()
        if i < len(jobs):
            kind, h, row = jobs[i]
            (issue_adapters if kind == "a" else issue_gradients)(h, row)
        if 0 <= i - lag < len(jobs):
            kind, h, row = jobs[i - lag]
            x_hand_on((kind, h, row), rx[h] if kind == "a" else gr[h], row)
        if 0 <= i - finish_lag < len(jobs):
            kind, h, row = jobs[i - finish_lag]
            if kind == "g":
                finish_gradients(h, row)
        if i == 0:
            for copy in table_copies:
                copy.wait_recv()
    write_gradients(1)
    for copy in copies.all:
        copy.wait_send()
    store_gi.wait()
    assert copies.used == copy_count(ny, nz)


def step(ny, nz, activations, cotangent, down_adapters, up_adapters, block_persona, persona_slot):
    blocks = block_persona.shape[0]
    block = activations.shape[0] // blocks
    features = activations.shape[1]
    pers, rank = up_adapters.shape[:2]
    smem = pl.BlockSpec(memory_space=pltpu.SMEM)
    vmem = pl.BlockSpec(memory_space=pltpu.VMEM)
    anywhere = pl.BlockSpec(memory_space=pl.ANY)
    line = jax.ShapeDtypeStruct((1, 128), jnp.int32)
    req, blk_slot, slot_blk = pl.pallas_call(
        functools.partial(prep_kernel, ny, pers, blocks),
        out_shape=(line, line, line),
        in_specs=[smem, smem],
        out_specs=(smem, smem, smem),
        scratch_shapes=[pltpu.SMEM((128,), jnp.int32)],
    )(block_persona, persona_slot)

    unit = CORES * nz * 16
    pad_blocks = blocks
    while pad_blocks * rank % unit:
        pad_blocks += 1
    rows = pad_blocks * rank
    adapter = (rank, features)

    def bf16(*shape):
        return pltpu.VMEM(shape, BF16)

    def f32(*shape):
        return pltpu.VMEM(shape, F32)

    scratch = [bf16(blocks, block, features)] * 3
    scratch += [bf16(pers, *adapter)] * (2 * ny - 1)
    scratch += [bf16(10 * ny, *adapter)] * 2
    scratch += [bf16(ny, 3, *adapter)] * 4
    scratch += [bf16(blocks + 1, *adapter)] * 2
    scratch += [bf16(8 * ny, *adapter)] * 2
    scratch += [bf16(ny, 3, *adapter)] * 4
    scratch += [bf16(pers, *adapter)] * (4 * (ny - 1))
    scratch += [f32(rows, block)] * 2 + [f32(rows // 2, block)] * 2
    scratch += [bf16(rows // 2, block)] * 2
    scratch += [bf16(max(nz - 1, 1), rows // 2 // nz, block)] * 2
    scratch += [bf16(rows, block)] * 2
    scratch += [
        pltpu.VMEM((NX, 1, 128), jnp.int32),
        pltpu.SMEM((NX, 1, 128), jnp.int32),
        pltpu.VMEM((ny, NX, 1, 128), jnp.int32),
    ]
    n = copy_count(ny, nz)
    scratch += [pltpu.SemaphoreType.DMA((n,)), pltpu.SemaphoreType.DMA((n,)), pltpu.SemaphoreType.DMA((4,))]
    gi, gdn, gup = pl.pallas_call(
        functools.partial(main_kernel, (ny, nz, pers, blocks, pad_blocks, rank)),
        out_shape=(
            jax.ShapeDtypeStruct((blocks, block, features), BF16),
            jax.ShapeDtypeStruct(down_adapters.shape, BF16),
            jax.ShapeDtypeStruct(up_adapters.shape, BF16),
        ),
        in_specs=[smem, smem, smem, vmem, vmem, vmem, anywhere, anywhere],
        out_specs=(anywhere, vmem, vmem),
        scratch_shapes=scratch,
        compiler_params=pltpu.CompilerParams(
            collective_id=0, has_side_effects=True, vmem_limit_bytes=56 * 2**20
        ),
    )(
        req, blk_slot, slot_blk, req, up_adapters, down_adapters,
        activations.reshape(blocks, block, features), cotangent.reshape(blocks, block, features),
    )
    return gi.reshape(activations.shape), gdn, gup


def solution(mesh):
    ny, nz = mesh.shape["dp"] // NX, mesh.shape["tensor"] // CORES
    return jax.shard_map(
        functools.partial(step, ny, nz),
        mesh=mesh,
        in_specs=(
            P("dp", "tensor"),
            P("dp", "tensor"),
            P("dp", "tensor", None),
            P("dp", None, "tensor"),
            P("dp"),
            P(),
        ),
        out_specs=(P("dp", "tensor"), P("dp", "tensor", None), P("dp", None, "tensor")),
        check_vma=False,
    )
```

time: 451 us -> 162 us (0.36)
  the two profiles are of different devices: /device:TPU:195 before, /device:TPU:64 now
where the time goes in v1:
time: 162 us
  Pallas kernels  154 us (95%)
  local copies, waits for them, and re-layouts  6.95 us (4%)
    pallas_call x1, Pallas kernels, step(): pl.pallas_call(functools.partial(main_kernel, (ny, nz, pers, blocks, pad_...  151 us
    unnamed x6, local copies, waits for them, and re-layouts  6.95 us

profile of v1, /device:TPU:64, one launch (start us, length us, event | category | flops | bytes accessed | tf_op | source)
XLA Modules:
  0.0 162.1 jit_solution(14662529918633881795)
XLA Ops:
  0.6 3.1 %shard_map.85 = (s32[1,128]{1,0:T(1,128)}, s32[1,128]{1,0:T(1,128)}, s32[1,128]{1,0:T(1,128)}) custom-call(s32[22]{0:T(128)} %bp.1, s32[192]{0:T(256)} %ps.1), custom_call_target="tpu_custom_call" | custom-call | tf_op jit(solution)/shard_map/pallas_call | solution.py:475
  3.7 1.9 %copy.9.refs_5_ = bf16[6,256,64]{2,1,0:T(8,128)(2,1)} copy(bf16[6,256,64]{1,2,0:T(8,128)(2,1)} %param.8) | data formatting | bytes 393216 | tf_op args[2]
  5.6 151.4 %shard_map.86 = (bf16[22,128,256]{2,1,0:T(8,128)(2,1)}, bf16[6,256,64]{2,1,0:T(8,128)(2,1)}, bf16[6,64,256]{2,1,0:T(8,128)(2,1)}) custom-call(s32[1,128]{1,0:T(1,128)} %get-tuple-element.9.refs_0_.refs_3_, s32[1,128]{1,0:T(1,128)} %get-tuple-element.10.refs_1_, s32[1,128]{1,0:T(1,128)} %get-tuple-element.11.refs_2_, ...), custom_call_target="tpu_custom_call" | custom-call | tf_op jit(solution)/shard_map/pallas_call | solution.py:515
  157.0 1.8 %copy.10 = bf16[6,256,64]{1,2,0:T(8,128)(2,1)} copy(bf16[6,256,64]{2,1,0:T(8,128)(2,1)} %get-tuple-element.16) | data formatting | bytes 393216
  158.8 0.0 copy-start
  158.8 2.6 %copy.13 = bf16[2816,256]{1,0:T(8,128)(2,1)} copy(bf16[2816,256]{1,0:T(8,128)(2,1)} %bitcast.5) | data formatting | bytes 2883584
  161.4 0.0 copy-done
  161.4 0.7 copy.14
Async XLA Ops:
  158.8 2.6 %copy-start = (bf16[6,64,256]{2,1,0:T(8,128)(2,1)S(1)}, bf16[6,64,256]{2,1,0:T(8,128)(2,1)}, u32[]{:S(2)}) copy-start(bf16[6,64,256]{2,1,0:T(8,128)(2,1)} %get-tuple-element.23) | copy-start | bytes 589828

commit v2 on v1

v2 whole, which is shorter than its diff:
```python
import functools

import jax
import jax.numpy as jnp
from jax import lax
from jax.experimental import pallas as pl
from jax.experimental.pallas import tpu as pltpu
from jax.sharding import PartitionSpec as P

MESH = pl.DeviceIdType.MESH
NX = 4
CORES = 2
CAP = 2
CHUNKS = 2
ADAPTER_SCALE = 2.0
F32 = jnp.float32
BF16 = jnp.bfloat16


class Copies:
    def __init__(self, send, recv):
        self.send, self.recv, self.used, self.all = send, recv, 0, []

    def make(self, src, dst, device):
        i = self.used
        self.used += 1
        copy = pltpu.make_async_remote_copy(
            src_ref=src, dst_ref=dst, send_sem=self.send.at[i], recv_sem=self.recv.at[i],
            device_id=device, device_id_type=MESH,
        )
        self.all.append(copy)
        return copy

    def flush(self, count):
        for copy in self.all[:count]:
            copy.wait_send()
        self.all = self.all[count:]


def copy_count(ny, nz):
    return 4 * ny * (NX - 1) + 4 * (ny - 1) * CHUNKS + 2 * (2 + 2 * (nz - 1)) + (NX - 1) + (ny - 1)


def main_kernel(cfg, *refs):
    ny, nz, pers, blocks, pad_blocks, rank = cfg
    (bp, ps, up_in, down_in, act, cot, gi, gdn, gup) = refs[:9]
    refs = list(refs[9:])

    def take(n):
        out = refs[:n]
        del refs[:n]
        return out

    act_v, cot_v, gi_v = take(3)
    tab = [take(ny), take(ny)]
    rx = take(2)
    sx = [take(NX - 1), take(NX - 1)]
    grads = take(2)
    gr = take(2)
    bs = [take(NX - 1), take(NX - 1)]
    ys = [take(ny - 1), take(ny - 1)]
    yr = [take(ny - 1), take(ny - 1)]
    part, pair, zs, zr, full = take(2), take(2), take(2), take(2), take(2)
    rtab_v, rtab_s, ctab, asked_v, asked_s, blk_slot = take(6)
    send_sem, recv_sem, local_sem = take(3)
    copies = Copies(send_sem, recv_sem)

    dp, tensor = lax.axis_index("dp"), lax.axis_index("tensor")
    y, x = dp // NX, lax.rem(dp, NX)
    z, core = tensor // CORES, lax.rem(tensor, CORES)

    def at_x(d):
        return (y * NX + lax.rem(x + d + NX, NX), tensor)

    def at_y(d):
        return (lax.rem(y + d + ny, ny) * NX + x, tensor)

    def at_z(d):
        return (dp, lax.rem(z + d + nz, nz) * CORES + core)

    sibling = (dp, z * CORES + (1 - core))

    load_act = pltpu.make_async_copy(act, act_v, local_sem.at[0])
    load_cot = pltpu.make_async_copy(cot, cot_v, local_sem.at[1])
    load_up = pltpu.make_async_copy(up_in, tab[0][0], local_sem.at[4])
    load_down = pltpu.make_async_copy(down_in, tab[1][0], local_sem.at[5])
    load_up.start()
    load_down.start()
    load_cot.start()
    load_act.start()

    barrier = pltpu.get_barrier_semaphore()
    peers = [at_x(d) for d in range(1, NX)] + [at_y(d) for d in range(1, ny)]
    peers += [at_z(d) for d in range(1, nz)] + [sibling]
    for peer in peers:
        pl.semaphore_signal(barrier, inc=1, device_id=peer, device_id_type=MESH)

    lane = lax.broadcasted_iota(jnp.int32, (1, 128), 1)
    req = jnp.full((1, 128), -1, jnp.int32)
    asked = jnp.full((1, 128), blocks, jnp.int32)
    owners = []
    for b in range(blocks):
        persona = jnp.clip(bp[b], 0, ps.shape[0] - 1)
        slot = jnp.clip(ps[persona], 0, ps.shape[0] - 1)
        owner = lax.div(slot, pers)
        pos = sum([(owner == other).astype(jnp.int32) for other in owners], jnp.int32(0))
        pos = jnp.minimum(pos, CAP - 1)
        owners.append(owner)
        here = lane == owner * CAP + pos
        req = jnp.where(here, slot - owner * pers, req)
        asked = jnp.where(here, b, asked)
        owner_y = lax.div(owner, NX)
        rel_y = lax.rem(owner_y - y + ny, ny)
        rel_x = lax.rem(owner - owner_y * NX - x + NX, NX)
        blk_slot[b] = (rel_x * ny + rel_y) * CAP + pos
    rtab_v[0] = req
    asked_v[...] = asked
    ask_to_smem = pltpu.make_async_copy(asked_v, asked_s, local_sem.at[6])
    ask_to_smem.start()

    pl.semaphore_wait(barrier, len(peers))

    steps_p = [ny // 2, ny - 1 - ny // 2]
    steps_m = [ny - 1 - ny // 2, ny // 2]
    ring = {}
    cut = pers // CHUNKS
    parts = [pl.ds(c * cut, cut if c < CHUNKS - 1 else pers - c * cut) for c in range(CHUNKS)]

    def ring_send(h, toward_low, step, c):
        if toward_low:
            src, row, device = tab[h][step - 1], step, at_y(-1)
        else:
            src, row, device = tab[h][(ny - step + 1) % ny], ny - step, at_y(1)
        copy = copies.make(src.at[parts[c]], tab[h][row].at[parts[c]], device)
        copy.start()
        ring[h, toward_low, step, c] = copy

    def ring_steps(h, toward_low):
        return (steps_p if toward_low else steps_m)[h]

    def ring_first(h, toward_low, c):
        if ring_steps(h, toward_low) >= 1:
            ring_send(h, toward_low, 1, c)

    def ring_take(h, step):
        for c in range(CHUNKS):
            for toward_low in (True, False):
                if step > ring_steps(h, toward_low):
                    continue
                ring[h, toward_low, step, c].wait_recv()
                if step < ring_steps(h, toward_low):
                    ring_send(h, toward_low, step + 1, c)
                if h == 0 and step == max(ring_steps(0, toward_low) - 1, 1):
                    ring_first(1, toward_low, c)
        low = [step] if step <= ring_steps(h, True) else []
        return low + ([ny - step] if step <= ring_steps(h, False) else [])

    ask = []
    for d in range(1, NX):
        copy = copies.make(rtab_v.at[0], rtab_v.at[NX - d], at_x(d))
        copy.start()
        ask.append(copy)
    load_up.wait()
    load_down.wait()
    for c in range(CHUNKS):
        ring_first(0, True, c)
        ring_first(0, False, c)
        if steps_m[0] == 0:
            ring_first(1, False, c)
    for copy in ask:
        copy.wait_recv()
    to_smem = pltpu.make_async_copy(rtab_v, rtab_s, local_sem.at[2])
    to_smem.start()
    ctab[0] = rtab_v[...]
    to_smem.wait()
    ask_to_smem.wait()
    table_copies = []
    for d in range(1, ny):
        copy = copies.make(rtab_v, ctab.at[ny - d], at_y(d))
        copy.start()
        table_copies.append(copy)

    def owner_slot(row, rel_x):
        return (lax.rem(y + row, ny) * NX + lax.rem(x + rel_x, NX)) * CAP

    hops = {}

    def land_at(rel_x, row):
        return pl.ds((rel_x * ny + row) * CAP, CAP)

    def x_send(key, land, stage, row):
        for d in (2, 1, 3):
            copy = copies.make(stage[d - 1].at[row], land.at[land_at(NX - d, row)], at_x(d))
            copy.start()
            hops[key, d] = copy

    def x_landed(key):
        for d in range(1, NX):
            hops[key, d].wait_recv()

    def issue_adapters(h, row):
        table = tab[h][row]

        def pick(rel_x, pos):
            return table[jnp.maximum(rtab_s[rel_x, 0, owner_slot(row, 0) + pos], 0)]

        for d in range(1, NX):
            for pos in range(CAP):
                sx[h][d - 1][row, pos] = pick(d, pos)
        x_send(("a", h, row), rx[h], sx[h], row)
        for pos in range(CAP):
            rx[h][row * CAP + pos] = pick(0, pos)

    def issue_gradients(h, row):
        for d in range(1, NX):
            for pos in range(CAP):
                bs[h][d - 1][row, pos] = grads[h][asked_s[0, owner_slot(row, d) + pos]]
        x_send(("g", h, row), gr[h], bs[h], row)

    sums = {}

    def row_sum(h, row, k):
        base = owner_slot(row, 0)
        total = jnp.zeros((rank, gup.shape[2]), F32)
        terms = []
        for rel_x in range(1, NX):
            for pos in range(CAP):
                place = (rel_x * ny + row) * CAP + pos
                terms.append((rtab_s[rel_x, 0, base + pos], gr[h][place]))
        for pos in range(CAP):
            terms.append((rtab_s[0, 0, base + pos], grads[h][asked_s[0, base + pos]]))
        for asked, term in terms:
            total += jnp.where(asked == k, term.astype(F32), 0.0)
        return total

    back_p = [steps_p[1], steps_p[0]]
    back_m = [steps_m[1], steps_m[0]]

    def back_place(h, row):
        j = ny - row
        return (True, j) if j <= back_p[h] else (False, row)

    def back_slot(toward_low, j):
        return j - 1 if toward_low else ny - 1 - j

    def back_order(h):
        order = []
        for j in range(ny // 2, 0, -1):
            order += [ny - j] if j <= back_p[h] else []
            order += [j] if j <= back_m[h] else []
        return order + [0]

    def finish_gradients(h, row):
        x_landed(("g", h, row))
        if row == 0:
            return
        toward_low, j = back_place(h, row)
        last = j == (back_p if toward_low else back_m)[h]
        farther = None if last else yr[h][back_slot(toward_low, j + 1)]
        out = ys[h][back_slot(toward_low, j)]
        land = yr[h][back_slot(toward_low, j)]

        def one(k, _):
            total = row_sum(h, row, k)
            if farther is not None:
                total += farther[k].astype(F32)
            out[k] = total.astype(BF16)
            return 0

        for c, part in enumerate(parts):
            if not last:
                sums[h, toward_low, j + 1, c].wait_recv()
            lax.fori_loop(part.start, part.start + part.size, one, 0)
            copy = copies.make(out.at[part], land.at[part], at_y(-1 if toward_low else 1))
            copy.start()
            sums[h, toward_low, j, c] = copy

    def write_gradients(h):
        nearest = []
        for toward_low in (True, False):
            if (back_p if toward_low else back_m)[h] >= 1:
                for c in range(CHUNKS):
                    sums[h, toward_low, 1, c].wait_recv()
                nearest.append(yr[h][back_slot(toward_low, 1)])
        mine = lane // CAP == dp
        for k in range(pers):
            hits = jnp.zeros((1, 128), F32)
            for other in range(ny):
                for rel_x in range(NX):
                    hits += jnp.where(mine & (ctab[other, rel_x] == k), 1.0, 0.0)
            count = jnp.sum(hits, axis=1, keepdims=True)
            scaling = ADAPTER_SCALE / (act.shape[1] * jnp.maximum(count, 1.0))
            total = row_sum(h, 0, k)
            for ref in nearest:
                total += ref[k].astype(F32)
            total = total * scaling
            if h == 0:
                gdn[k] = total.astype(BF16)
            else:
                gup[k] = total.astype(BF16)

    half = pad_blocks * rank // 2
    chunk = half // nz
    tensor_copies = {}

    def rows_of(c, zz):
        return pl.ds(pl.multiple_of(c * half + zz * chunk, 16), chunk)

    def project(h):
        if h == 0:
            load_cot.wait()
        for row in range(ny):
            x_landed(("a", h, row))
        tokens = cot_v if h == 0 else act_v

        def one(b, _):
            weights = rx[h][blk_slot[b]]
            part[h][pl.ds(pl.multiple_of(b * rank, rank), rank), :] = lax.dot_general(
                weights, tokens[b], (((1,), (1,)), ((), ())), preferred_element_type=F32
            )
            return 0

        lax.fori_loop(0, blocks, one, 0, unroll=2)
        if pad_blocks > blocks:
            part[h][pl.ds(blocks * rank, (pad_blocks - blocks) * rank), :] = jnp.zeros(
                ((pad_blocks - blocks) * rank, part[h].shape[1]), F32
            )
        copy = copies.make(
            part[h].at[pl.ds(pl.multiple_of((1 - core) * half, 16), half)], pair[h], sibling
        )
        copy.start()
        tensor_copies[h, "pair"] = copy

    def scatter(h):
        tensor_copies[h, "pair"].wait_recv()

        def one(zz, _):
            rows = pl.ds(pl.multiple_of(zz * chunk, 16), chunk)
            zs[h][rows, :] = (part[h][rows_of(core, zz), :] + pair[h][rows, :]).astype(BF16)
            return 0

        lax.fori_loop(0, nz, one, 0)
        for d in range(1, nz):
            other = lax.rem(z + d, nz)
            copy = copies.make(
                zs[h].at[pl.ds(pl.multiple_of(other * chunk, 16), chunk)], zr[h].at[d - 1], at_z(d)
            )
            copy.start()
            tensor_copies[h, "scatter", d] = copy

    def gather(h):
        own = pl.ds(pl.multiple_of(z * chunk, 16), chunk)
        total = part[h][rows_of(core, z), :] + pair[h][own, :]
        for d in range(1, nz):
            tensor_copies[h, "scatter", d].wait_recv()
            total += zr[h][d - 1].astype(F32)
        mine = rows_of(core, z)
        full[h][mine, :] = total.astype(BF16)
        for d in range(1, nz):
            copy = copies.make(full[h].at[mine], full[h].at[mine], at_z(d))
            copy.start()
            tensor_copies[h, "gather", d] = copy

    def share(h):
        for d in range(1, nz):
            tensor_copies[h, "gather", d].wait_recv()
        mine = pl.ds(pl.multiple_of(core * half, 16), half)
        copy = copies.make(full[h].at[mine], full[h].at[mine], sibling)
        copy.start()
        tensor_copies[h, "share"] = copy

    def ranks(h, b):
        return full[h][pl.ds(pl.multiple_of(b * rank, rank), rank), :]

    def block_gradients(h):
        tensor_copies[h, "share"].wait_recv()
        if h == 0:
            load_act.wait()
        tokens = act_v if h == 0 else cot_v
        grads[h][blocks] = jnp.zeros(grads[h].shape[1:], BF16)

        def one(b, _):
            grads[h][b] = jnp.dot(ranks(h, b), tokens[b], preferred_element_type=F32).astype(BF16)
            return 0

        lax.fori_loop(0, blocks, one, 0, unroll=2)

    store_gi = pltpu.make_async_copy(gi_v, gi, local_sem.at[3])

    def input_gradient():
        def one(b, _):
            weights = rx[1][blk_slot[b]]
            gi_v[b] = (
                ADAPTER_SCALE
                * lax.dot_general(
                    ranks(0, b), weights, (((0,), (0,)), ((), ())), preferred_element_type=F32
                )
            ).astype(BF16)
            return 0

        lax.fori_loop(0, blocks, one, 0, unroll=2)
        store_gi.start()

    issue_adapters(0, 0)
    for s in range(1, ny // 2 + 1):
        for row in ring_take(0, s):
            issue_adapters(0, row)
    issue_adapters(1, 0)
    for copy in table_copies:
        copy.wait_recv()
    beside = [(2, project), (3, scatter), (4, gather), (4, share), (99, block_gradients)]
    for s in range(1, ny // 2 + 1):
        for row in ring_take(1, s):
            issue_adapters(1, row)
        while s >= beside[0][0]:
            beside.pop(0)[1](0)
    for _, what in beside:
        what(0)
    early = len(copies.all)
    orders = [back_order(0), back_order(1)]
    for row in orders[0][: ny // 2]:
        issue_gradients(0, row)
    project(1)
    for row in orders[0][ny // 2 :]:
        issue_gradients(0, row)
    scatter(1)

    def turn():
        block_gradients(1)
        for row in orders[1]:
            issue_gradients(1, row)
        copies.flush(early)

    beside = [
        (1, lambda: gather(1)), (2, input_gradient), (3, lambda: share(1)), (4, turn),
    ]
    for i, row in enumerate(orders[0]):
        finish_gradients(0, row)
        while beside and i >= beside[0][0]:
            beside.pop(0)[1]()
    for _, what in beside:
        what()
    write_gradients(0)
    middle = len(copies.all)
    for i, row in enumerate(orders[1]):
        if i == ny - 2:
            copies.flush(middle)
        finish_gradients(1, row)
    write_gradients(1)
    copies.flush(len(copies.all))
    store_gi.wait()
    assert copies.used == copy_count(ny, nz)


def step(ny, nz, activations, cotangent, down_adapters, up_adapters, block_persona, persona_slot):
    blocks = block_persona.shape[0]
    block = activations.shape[0] // blocks
    features = activations.shape[1]
    pers, rank = up_adapters.shape[:2]
    smem = pl.BlockSpec(memory_space=pltpu.SMEM)
    vmem = pl.BlockSpec(memory_space=pltpu.VMEM)
    anywhere = pl.BlockSpec(memory_space=pl.ANY)
    unit = CORES * nz * 16
    pad_blocks = blocks
    while pad_blocks * rank % unit:
        pad_blocks += 1
    rows = pad_blocks * rank
    adapter = (rank, features)

    def bf16(*shape):
        return pltpu.VMEM(shape, BF16)

    def f32(*shape):
        return pltpu.VMEM(shape, F32)

    scratch = [bf16(blocks, block, features)] * 3
    landing = NX * ny * CAP
    scratch += [bf16(pers, *adapter)] * (2 * ny)
    scratch += [bf16(landing, *adapter)] * 2
    scratch += [bf16(ny, CAP, *adapter)] * (2 * (NX - 1))
    scratch += [bf16(blocks + 1, *adapter)] * 2
    scratch += [bf16(landing, *adapter)] * 2
    scratch += [bf16(ny, CAP, *adapter)] * (2 * (NX - 1))
    scratch += [bf16(pers, *adapter)] * (4 * (ny - 1))
    scratch += [f32(rows, block)] * 2 + [f32(rows // 2, block)] * 2
    scratch += [bf16(rows // 2, block)] * 2
    scratch += [bf16(max(nz - 1, 1), rows // 2 // nz, block)] * 2
    scratch += [bf16(rows, block)] * 2
    scratch += [
        pltpu.VMEM((NX, 1, 128), jnp.int32),
        pltpu.SMEM((NX, 1, 128), jnp.int32),
        pltpu.VMEM((ny, NX, 1, 128), jnp.int32),
        pltpu.VMEM((1, 128), jnp.int32),
        pltpu.SMEM((1, 128), jnp.int32),
        pltpu.SMEM((blocks,), jnp.int32),
    ]
    n = copy_count(ny, nz)
    scratch += [pltpu.SemaphoreType.DMA((n,)), pltpu.SemaphoreType.DMA((n,)), pltpu.SemaphoreType.DMA((7,))]
    gi, gdn, gup = pl.pallas_call(
        functools.partial(main_kernel, (ny, nz, pers, blocks, pad_blocks, rank)),
        out_shape=(
            jax.ShapeDtypeStruct((blocks, block, features), BF16),
            jax.ShapeDtypeStruct(up_adapters.shape, BF16),
            jax.ShapeDtypeStruct(up_adapters.shape, BF16),
        ),
        in_specs=[smem, smem] + [anywhere] * 4,
        out_specs=(anywhere, vmem, vmem),
        scratch_shapes=scratch,
        compiler_params=pltpu.CompilerParams(
            collective_id=0, has_side_effects=True, vmem_limit_bytes=56 * 2**20
        ),
    )(
        block_persona, persona_slot, up_adapters, jnp.swapaxes(down_adapters, 1, 2),
        activations.reshape(blocks, block, features), cotangent.reshape(blocks, block, features),
    )
    return gi.reshape(activations.shape), jnp.swapaxes(gdn, 1, 2), gup


def solution(mesh):
    ny, nz = mesh.shape["dp"] // NX, mesh.shape["tensor"] // CORES
    return jax.shard_map(
        functools.partial(step, ny, nz),
        mesh=mesh,
        in_specs=(
            P("dp", "tensor"),
            P("dp", "tensor"),
            P("dp", "tensor", None),
            P("dp", None, "tensor"),
            P("dp"),
            P(),
        ),
        out_specs=(P("dp", "tensor"), P("dp", "tensor", None), P("dp", None, "tensor")),
        check_vma=False,
    )
```

time: 162 us -> 127 us (0.78)
  the two profiles are of different devices: /device:TPU:64 before, /device:TPU:1 now
where the time goes in v2:
time: 127 us
  Pallas kernels  123 us (97%)
  local copies, waits for them, and re-layouts  3.97 us (3%)
    pallas_call x1, Pallas kernels, step(): pl.pallas_call(functools.partial(main_kernel, (ny, nz, pers, blocks, pad_...  123 us
    unnamed x7, local copies, waits for them, and re-layouts  3.97 us

profile of v2, /device:TPU:1, one launch (start us, length us, event | category | flops | bytes accessed | tf_op | source)
XLA Modules:
  0.0 127.2 jit_solution(12525790325676500060)
XLA Ops:
  0.6 122.6 %shard_map.85 = (bf16[22,128,256]{2,1,0:T(8,128)(2,1)}, bf16[6,64,256]{2,1,0:T(8,128)(2,1)}, bf16[6,64,256]{2,1,0:T(8,128)(2,1)}) custom-call(s32[22]{0:T(128)} %refs_0_.1, s32[192]{0:T(256)} %refs_1_.1, bf16[6,64,256]{2,1,0:T(8,128)(2,1)} %refs_2_.1, bf16[6,64,256]{2,1,0:T(8,128)(2,1)} %bitcast.8, bf16[22,128,256]{2,1,0:T(8,128)(2,1)} %bitcast.5, ...), custom_call_target="tpu_custom_call" | custom-call | tf_op jit(solution)/shard_map/pallas_call | solution.py:499
  123.2 0.0 copy-start.1
  123.2 0.0 copy-start
  123.3 2.6 %copy.12 = bf16[2816,256]{1,0:T(8,128)(2,1)} copy(bf16[2816,256]{1,0:T(8,128)(2,1)} %bitcast.7) | data formatting | bytes 2883584
  125.9 0.0 copy-done.1
  125.9 0.7 copy.13
  126.5 0.0 copy-done
  126.5 0.7 copy.14
Async XLA Ops:
  123.2 2.6 %copy-start.1 = (bf16[6,64,256]{2,1,0:T(8,128)(2,1)S(1)}, bf16[6,64,256]{2,1,0:T(8,128)(2,1)}, u32[]{:S(2)}) copy-start(bf16[6,64,256]{2,1,0:T(8,128)(2,1)} %get-tuple-element.7) | copy-start | bytes 589828
  123.2 3.3 %copy-start = (bf16[6,64,256]{2,1,0:T(8,128)(2,1)S(1)}, bf16[6,64,256]{2,1,0:T(8,128)(2,1)}, u32[]{:S(2)}) copy-start(bf16[6,64,256]{2,1,0:T(8,128)(2,1)} %get-tuple-element.14) | copy-start | bytes 589828

commit v3 on v2

--- a/solution.py
+++ b/solution.py
@@ -38,7 +38,7 @@
 
 
 def copy_count(ny, nz):
-    return 4 * ny * (NX - 1) + 4 * (ny - 1) * CHUNKS + 2 * (2 + 2 * (nz - 1)) + (NX - 1) + (ny - 1)
+    return 4 * ny * (NX - 1) + 4 * (ny - 1) * CHUNKS + 2 * (1 + nz + 2 * (nz - 1)) + (NX - 1) + (ny - 1)
 
 
 def main_kernel(cfg, *refs):
@@ -360,20 +360,25 @@
             copy = copies.make(full[h].at[mine], full[h].at[mine], at_z(d))
             copy.start()
             tensor_copies[h, "gather", d] = copy
+        share_chunk(h, 0)
+
+    def share_chunk(h, d):
+        rows = rows_of(core, lax.rem(z - d + nz, nz))
+        copy = copies.make(full[h].at[rows], full[h].at[rows], sibling)
+        copy.start()
+        tensor_copies[h, "share", d] = copy
 
     def share(h):
         for d in range(1, nz):
             tensor_copies[h, "gather", d].wait_recv()
-        mine = pl.ds(pl.multiple_of(core * half, 16), half)
-        copy = copies.make(full[h].at[mine], full[h].at[mine], sibling)
-        copy.start()
-        tensor_copies[h, "share"] = copy
+            share_chunk(h, d)
 
     def ranks(h, b):
         return full[h][pl.ds(pl.multiple_of(b * rank, rank), rank), :]
 
     def block_gradients(h):
-        tensor_copies[h, "share"].wait_recv()
+        for d in range(nz):
+            tensor_copies[h, "share", d].wait_recv()
         if h == 0:
             load_act.wait()
         tokens = act_v if h == 0 else cot_v

time: 127 us -> 127 us (level)
  the two profiles are of different devices: /device:TPU:1 before, /device:TPU:64 now
where the time goes in v3:
time: 127 us
  Pallas kernels  122 us (96%)
  local copies, waits for them, and re-layouts  3.97 us (3%)
    pallas_call x1, Pallas kernels, step(): pl.pallas_call(functools.partial(main_kernel, (ny, nz, pers, blocks, pad_...  122 us
    unnamed x7, local copies, waits for them, and re-layouts  3.97 us

profile of v3, /device:TPU:64, one launch (start us, length us, event | category | flops | bytes accessed | tf_op | source)
XLA Modules:
  0.0 126.6 jit_solution(406323237415121235)
XLA Ops:
  0.6 122.0 %shard_map.85 = (bf16[22,128,256]{2,1,0:T(8,128)(2,1)}, bf16[6,64,256]{2,1,0:T(8,128)(2,1)}, bf16[6,64,256]{2,1,0:T(8,128)(2,1)}) custom-call(s32[22]{0:T(128)} %refs_0_.1, s32[192]{0:T(256)} %refs_1_.1, bf16[6,64,256]{2,1,0:T(8,128)(2,1)} %refs_2_.1, bf16[6,64,256]{2,1,0:T(8,128)(2,1)} %bitcast.8, bf16[22,128,256]{2,1,0:T(8,128)(2,1)} %bitcast.5, ...), custom_call_target="tpu_custom_call" | custom-call | tf_op jit(solution)/shard_map/pallas_call | solution.py:504
  122.7 0.0 copy-start.1
  122.7 0.0 copy-start
  122.7 2.6 %copy.12 = bf16[2816,256]{1,0:T(8,128)(2,1)} copy(bf16[2816,256]{1,0:T(8,128)(2,1)} %bitcast.7) | data formatting | bytes 2883584
  125.3 0.0 copy-done.1
  125.3 0.7 copy.13
  126.0 0.0 copy-done
  126.0 0.7 copy.14
Async XLA Ops:
  122.7 2.6 %copy-start.1 = (bf16[6,64,256]{2,1,0:T(8,128)(2,1)S(1)}, bf16[6,64,256]{2,1,0:T(8,128)(2,1)}, u32[]{:S(2)}) copy-start(bf16[6,64,256]{2,1,0:T(8,128)(2,1)} %get-tuple-element.7) | copy-start | bytes 589828
  122.7 3.3 %copy-start = (bf16[6,64,256]{2,1,0:T(8,128)(2,1)S(1)}, bf16[6,64,256]{2,1,0:T(8,128)(2,1)}, u32[]{:S(2)}) copy-start(bf16[6,64,256]{2,1,0:T(8,128)(2,1)} %get-tuple-element.14) | copy-start | bytes 589828
